TPU v7x, 32 devices: a whole 2x2x4 slice. The times are simulated.
32 devices in a mesh: pitch: 2 (over x), blk: 16 (over z, y, core).
Axes of the slice: x: 2, y: 2, z: 4, core: 2. Of those that a mesh axis runs over, the one named last changes fastest.
Arguments:
- flux: float32 [128, 16, 45, 128], P('pitch', 'blk'), may hold values from -6 to 6
- pitch_inverse: float32 [16, 128, 128], P('blk', 'pitch')
- span_inverse: float32 [16, 128, 128], P('blk')
- store_old: bfloat16 [2, 16, 32, 45, 128], P('pitch', 'blk'), may hold values from -6 to 6
- send_row: int32 [2, 16, 16], P('pitch', 'blk'), may hold values from 0 to 63
- send_owner: int32 [2, 16, 16], P('pitch', 'blk'), may hold values from 0 to 15, as said below
- send_slot: int32 [2, 16, 16], P('pitch', 'blk'), may hold values from 0 to 31, as said below
- send_count: int32 [2, 16], P('pitch', 'blk'), may hold values from 8 to 16, as said below
Outputs:
- smoothed: float32 [128, 16, 45, 128], P('pitch', 'blk')
- storage: float32 [2, 16, 32, 45, 128], P('pitch', 'blk')
Inputs may be any that keep to these rules, and one draw needn't show every extreme that they name: Live entries are the first send_count of each list; in every draw some device has all 16 entries live. `send_owner`: among one device's live entries no owner is named more than 2 times; in every pitch group one owner is named 2 times by the live entries of every device. `send_slot`: within one pitch group, the live entries that name one owner carry distinct slots. `send_row`: the index is r = p * 1 + b on the sending device, with p its local pitch cell and b its local axial cell.
All inputs are finite; a program needn't handle non-finite values.
Results may differ from a plain program's by a relative error of at most 0.0003.
Values sent between devices are 32-bit elements; how exact they have to be, the bound alone decides.
A program may use at most 64 MiB of HBM per device.

v0:
```python
import jax
import jax.numpy as jnp
from jax import lax
from jax.sharding import PartitionSpec as P

CAP = 2


def with_halo(block, sides, width):
    for axis, dim in sides:
        count = lax.axis_size(axis)
        forward = [(i, i + 1) for i in range(count - 1)]
        backward = [(target, source) for source, target in forward]
        low = lax.ppermute(
            lax.slice_in_dim(block, block.shape[dim] - width, None, axis=dim), axis, forward
        )
        high = lax.ppermute(lax.slice_in_dim(block, 0, width, axis=dim), axis, backward)
        block = jnp.concatenate([low, block, high], axis=dim)
    return block


def local(
    flux, pitch_inverse, span_inverse, store_old, send_row, send_owner, send_slot, send_count
):
    highest = lax.Precision.HIGHEST
    padded = with_halo(flux, (("blk", 1),), 1)
    residual = 0.25 * padded[:, 2:] - 0.75 * padded[:, :-2] + 0.5 * flux
    pitch_local, axial_local, components, span_cells = flux.shape
    flattened = residual.reshape(pitch_local, axial_local, components * span_cells)
    whole_rows = lax.all_gather(pitch_inverse, "pitch", axis=1, tiled=True)[0]
    offset = lax.axis_index("pitch") * pitch_local
    own_columns = lax.dynamic_slice_in_dim(whole_rows, offset, pitch_local, 1)
    pitch_smoothed = lax.psum_scatter(
        jnp.einsum("pk,kbx->pbx", own_columns, flattened, precision=highest),
        "pitch",
        scatter_dimension=0,
        tiled=True,
    )
    pitch_smoothed = pitch_smoothed.reshape(pitch_local, axial_local, components, span_cells)
    smoothed = jnp.einsum("pbqs,ts->pbqt", pitch_smoothed, span_inverse[0], precision=highest)
    line_rows = smoothed.reshape(pitch_local * axial_local, components, span_cells)
    owners_total = lax.axis_size("blk")
    slot_total = store_old.shape[2]
    entries = send_owner.shape[2]
    owner_ids = send_owner[0, 0]
    is_live = jnp.arange(entries, dtype=jnp.int32) < send_count[0, 0]
    matches = (owner_ids[:, None] == jnp.arange(owners_total, dtype=jnp.int32)[None, :]).astype(
        jnp.int32
    )
    order_rank = jnp.sum(jnp.cumsum(matches, axis=0) * matches, axis=1) - 1
    target = jnp.where(is_live, owner_ids * CAP + order_rank, owners_total * CAP)
    outgoing = jnp.zeros((owners_total * CAP, components, span_cells), jnp.float32)
    outgoing = outgoing.at[target].set(line_rows[send_row[0, 0]], mode="drop")
    slot_tags = (
        jnp.full((owners_total * CAP,), slot_total, jnp.int32)
        .at[target]
        .set(send_slot[0, 0], mode="drop")
    )
    arrived, arrived_tags = (
        lax.all_to_all(
            outgoing.reshape(owners_total, CAP, components, span_cells),
            "blk",
            split_axis=0,
            concat_axis=0,
            tiled=True,
        ),
        lax.all_to_all(
            slot_tags.reshape(owners_total, CAP), "blk", split_axis=0, concat_axis=0, tiled=True
        ),
    )
    storage = (
        store_old[0, 0]
        .astype(jnp.float32)
        .at[arrived_tags.reshape(-1)]
        .set(arrived.reshape(-1, components, span_cells), mode="drop")
    )
    return (smoothed, storage[None, None])


def solution(mesh):
    return jax.shard_map(
        local,
        mesh=mesh,
        in_specs=(
            P("pitch", "blk", None, None),
            P("blk", "pitch", None),
            P("blk", None, None),
            P("pitch", "blk", None, None, None),
            P("pitch", "blk", None),
            P("pitch", "blk", None),
            P("pitch", "blk", None),
            P("pitch", "blk"),
        ),
        out_specs=(P("pitch", "blk", None, None), P("pitch", "blk", None, None, None)),
        check_vma=False,
    )
```

profile of v0, /device:TPU:25, one launch (start us, length us, event | category | flops | bytes accessed | tf_op | source)
XLA Modules:
  0.0 147.8 jit_solution(15483108445783796699)
XLA Ops:
  7.2 0.0 copy-start
  7.2 0.0 reduce-scatter.2.cloned.1.call-start
  7.2 2.6 %collective-permute-start = (f32[64,1,45,128]{3,1,2,0:T(1,128)}, f32[64,1,45,128]{3,1,2,0:T(1,128)S(1)}, u32[]{:S(2)}, u32[]{:S(2)}) collective-permute-start(f32[64,1,45,128]{3,1,2,0:T(1,128)} %param.8), channel_id=1, source_target_pairs={{1,0},{2,1},{3,2},{4,3},{5,4},{6,5},{7,6},{8,7},{9,8},{10,9},{11,1... | collective-permute-start | bytes 4423688 | tf_op jit(solution)/shard_map/ppermute | solution.py:17
  9.8 3.0 %collective-permute-start.1 = (f32[64,1,45,128]{3,1,2,0:T(1,128)}, f32[64,1,45,128]{3,1,2,0:T(1,128)S(1)}, u32[]{:S(2)}, u32[]{:S(2)}) collective-permute-start(f32[64,1,45,128]{3,1,2,0:T(1,128)} %param.8), channel_id=1, source_target_pairs={{0,1},{1,2},{2,3},{3,4},{4,5},{5,6},{6,7},{7,8},{8,9},{9,10},{10,1... | collective-permute-start | bytes 4423688 | tf_op jit(solution)/shard_map/ppermute | solution.py:14
  12.9 4.1 %all_gather.3 = f32[1,128,128]{2,1,0:T(8,128)S(1)} all-gather(f32[1,64,128]{2,1,0:T(8,128)} %param.9), channel_id=1, replica_groups=mesh['pitch'=2,'blk'=16] {'pitch'}, dimensions={1}, use_global_device_ids=true | all-gather | bytes 98304 | tf_op jit(solution)/shard_map/all_gather | solution.py:30
  17.0 27.0 %collective-permute-done = f32[64,1,45,128]{3,1,2,0:T(1,128)S(1)} collective-permute-done((f32[64,1,45,128]{3,1,2,0:T(1,128)}, f32[64,1,45,128]{3,1,2,0:T(1,128)S(1)}, u32[]{:S(2)}, u32[]{:S(2)}) %collective-permute-start) | collective-permute-done | bytes 1474592 | tf_op jit(solution)/shard_map/ppermute | solution.py:17
  44.0 0.0 collective-permute-done.1
  44.0 16.3 %add_reduce_fusion = f32[64,45,128]{2,1,0:T(8,128)S(1)} fusion(f32[64,1,45,128]{3,1,2,0:T(1,128)} %param.8, f32[64,1,45,128]{3,1,2,0:T(1,128)S(1)} %collective-permute-done.1, f32[64,1,45,128]{3,1,2,0:T(1,128)S(1)} %collective-permute-done), kind=kLoop, calls=%fused_computation.9 | loop fusion | flops 1843200 | bytes 5898240 | tf_op jit(solution)/shard_map/add | solution.py:27
  60.3 4.3 %convolution_bitcast_fusion = f32[128,1,5760]{2,0,1:T(8,128)} fusion(f32[8,8,45,128]{3,2,1,0:T(8,128)S(1)} %bitcast.47, f32[1,128,128]{2,1,0:T(8,128)S(1)} %all_gather.3, s32[]{:T(128)S(6)} %select_n.45), kind=kOutput, calls=%fused_computation.4 | convolution fusion | flops 566231040 | bytes 4489220 | tf_op jit(solution)/shard_map/pk,kbx->pbx/dot_general | solution.py:34
  64.6 0.0 copy-start.2
  64.6 0.0 copy-start.3
  64.6 0.0 reduce-scatter.2.cloned.1.call-update
  64.6 0.6 copy-done.2
  65.3 0.1 fusion.7
  66.0 0.2 select_reduce_fusion
  66.2 0.8 scatter_custom_fusion
  67.0 0.7 all_to_all.9
  67.7 6.2 %all-to-all-start = ((s32[16,1,2]{2,1,0:T(1,128)}), s32[16,1,2]{2,1,0:T(1,128)S(1)}, u32[]{:S(2)}, u32[]{:S(2)}) async-start(s32[16,1,2]{2,1,0:T(1,128)} %bitcast.12), calls=%async_computation.1 | async-start | bytes 16384 | tf_op jit(solution)/shard_map/all_to_all | solution.py:67
  73.9 0.0 copy-done.3
  73.9 32.9 %reduce-scatter.2.cloned.1.call-done = f32[64,1,5760]{2,0,1:T(8,128)} async-done(((f32[128,1,5760]{2,0,1:T(8,128)}), f32[64,1,5760]{2,0,1:T(8,128)}) %reduce-scatter.2.cloned.1.call-update) | async-done | bytes 1474576 | tf_op jit(solution)/shard_map/reduce_scatter | solution.py:33
  106.8 1.5 %reshape.136 = f32[64,45,128]{2,1,0:T(8,128)S(1)} reshape(f32[64,1,5760]{2,0,1:T(8,128)} %reduce-scatter.2.cloned.1.call-done) | data formatting | bytes 2949120 | tf_op jit(solution)/shard_map/reshape.3
  108.3 0.0 copy-done
  108.3 1.6 %fusion.2 = f32[64,45,128]{2,0,1:T(8,128)S(1)} fusion(f32[64,45,128]{2,1,0:T(8,128)S(1)} %reshape.136, f32[1,128,128]{2,1,0:T(8,128)S(1)} %copy-done), kind=kOutput, calls=%fused_computation.7 | convolution fusion | flops 566231040 | bytes 3014656 | tf_op jit(solution)/shard_map/pbqs,ts->pbqt/dot_general | solution.py:40
  110.0 0.9 copy.27
  110.8 0.6 gather_fusion
  111.4 0.1 broadcast_in_dim.16
  111.5 1.2 scatter_fusion
  112.7 0.0 copy-start.1
  112.7 1.2 copy.28
  114.0 0.0 all-to-all-done
  114.0 6.3 %all-to-all-start.1 = ((f32[16,2,45,128]{3,1,2,0:T(2,128)}), f32[16,2,45,128]{3,1,2,0:T(2,128)S(1)}, u32[]{:S(2)}, u32[]{:S(2)}) async-start(f32[16,2,45,128]{3,1,2,0:T(2,128)} %copy.28), calls=%async_computation.2 | async-start | bytes 1474560 | tf_op jit(solution)/shard_map/all_to_all | solution.py:60
  120.3 0.0 copy-done.1
  120.3 0.1 bitcast_convert_fusion
  120.4 0.5 broadcast.120
  120.9 0.7 reduce.5
  121.6 0.1 reshape.137
  121.7 2.6 %copy.31 = f32[64,1,45,128]{3,1,2,0:T(1,128)} copy(f32[64,1,45,128]{3,0,2,1:T(8,128)S(1)} %bitcast.45) | data formatting | bytes 2949120
  124.3 12.7 %all-to-all-done.1 = f32[16,2,45,128]{3,1,2,0:T(2,128)S(1)} async-done(((f32[16,2,45,128]{3,1,2,0:T(2,128)}), f32[16,2,45,128]{3,1,2,0:T(2,128)S(1)}, u32[]{:S(2)}, u32[]{:S(2)}) %all-to-all-start.1) | async-done | bytes 737312 | tf_op jit(solution)/shard_map/all_to_all | solution.py:60
  137.0 0.4 copy.29
  137.4 0.4 copy.30
  137.9 1.9 %scatter_fusion.1 = f32[32,45,128]{2,1,0:T(8,128)S(1)} fusion(f32[32,45,128]{2,1,0:T(8,128)S(1)} %bitcast_convert_fusion, s32[32]{0:T(128)S(1)} %fusion.8, f32[32,45,128]{2,1,0:T(8,128)S(1)} %copy.30), kind=kCustom, calls=%fused_computation.3 | custom fusion | bytes 2211968 | tf_op jit(solution)/shard_map/scatter | solution.py:75
  139.8 1.1 copy.32
  (5 shorter events, 0.1 us)
Async XLA Ops:
  7.2 101.2 %copy-start = (f32[1,128,128]{2,1,0:T(8,128)S(1)}, f32[1,128,128]{2,1,0:T(8,128)}, u32[]{:S(2)}) copy-start(f32[1,128,128]{2,1,0:T(8,128)} %param.10) | copy-start | bytes 196612
  7.2 99.6 %reduce-scatter.2.cloned.1.call-start = ((), (), s32[]{:S(2)}) async-start(), calls=%async_computation.3 | async-start | bytes 4423680 | tf_op jit(solution)/shard_map/reduce_scatter | solution.py:33
  7.2 36.8 %collective-permute-start = (f32[64,1,45,128]{3,1,2,0:T(1,128)}, f32[64,1,45,128]{3,1,2,0:T(1,128)S(1)}, u32[]{:S(2)}, u32[]{:S(2)}) collective-permute-start(f32[64,1,45,128]{3,1,2,0:T(1,128)} %param.8), channel_id=1, source_target_pairs={{1,0},{2,1},{3,2},{4,3},{5,4},{6,5},{7,6},{8,7},{9,8},{10,9},{11,1... | collective-permute-start | bytes 4423688 | tf_op jit(solution)/shard_map/ppermute | solution.py:17
  9.8 34.2 %collective-permute-start.1 = (f32[64,1,45,128]{3,1,2,0:T(1,128)}, f32[64,1,45,128]{3,1,2,0:T(1,128)S(1)}, u32[]{:S(2)}, u32[]{:S(2)}) collective-permute-start(f32[64,1,45,128]{3,1,2,0:T(1,128)} %param.8), channel_id=1, source_target_pairs={{0,1},{1,2},{2,3},{3,4},{4,5},{5,6},{6,7},{7,8},{8,9},{9,10},{10,1... | collective-permute-start | bytes 4423688 | tf_op jit(solution)/shard_map/ppermute | solution.py:14
  64.6 0.7 copy-start.2
  64.6 9.3 %copy-start.3 = (s32[1,1,16]{2,1,0:T(1,128)S(1)}, s32[1,1,16]{2,1,0:T(1,128)}, u32[]{:S(2)}) copy-start(s32[1,1,16]{2,1,0:T(1,128)} %param.12) | copy-start | bytes 196
  67.7 46.3 %all-to-all-start = ((s32[16,1,2]{2,1,0:T(1,128)}), s32[16,1,2]{2,1,0:T(1,128)S(1)}, u32[]{:S(2)}, u32[]{:S(2)}) async-start(s32[16,1,2]{2,1,0:T(1,128)} %bitcast.12), calls=%async_computation.1 | async-start | bytes 16384 | tf_op jit(solution)/shard_map/all_to_all | solution.py:67
  112.7 7.6 %copy-start.1 = (bf16[1,1,32,45,128]{4,2,3,1,0:T(8,128)(2,1)S(1)}, bf16[1,1,32,45,128]{4,2,3,1,0:T(8,128)(2,1)}, u32[]{:S(2)}) copy-start(bf16[1,1,32,45,128]{4,2,3,1,0:T(8,128)(2,1)} %param.11) | copy-start | bytes 1105924
  114.0 23.1 %all-to-all-start.1 = ((f32[16,2,45,128]{3,1,2,0:T(2,128)}), f32[16,2,45,128]{3,1,2,0:T(2,128)S(1)}, u32[]{:S(2)}, u32[]{:S(2)}) async-start(f32[16,2,45,128]{3,1,2,0:T(2,128)} %copy.28), calls=%async_computation.2 | async-start | bytes 1474560 | tf_op jit(solution)/shard_map/all_to_all | solution.py:60
Sparse Core Ops, SparseCore 0:
  64.8 41.9 reduce-scatter.1
where the time goes:
time: 150 us; the launch traced here: 148 us
  waiting for transfers between devices  72.6 us (48%)
  starting transfers between devices  18.2 us (12%)
  other arithmetic  17.4 us (12%)
  between operations  14.9 us (10%)
  local copies, waits for them, and re-layouts  14.6 us (10%)
  matrix products  5.93 us (4%)
  blocking collectives  4.12 us (3%)
    reduce_scatter x1, waiting for transfers between devices, local(): lax.psum_scatter(jnp.einsum('pk,kbx->pbx', own_columns, flattened, precis...  32.9 us
    ppermute x1, waiting for transfers between devices, with_halo(): lax.ppermute(lax.slice_in_dim(block, 0, width, axis=dim), axis, backward)  27 us
    add x1, other arithmetic, local(): residual = 0.25 * padded[:, 2:] - 0.75 * padded[:, :-2] + 0.5 * flux  16.3 us
    all_to_all x1, waiting for transfers between devices, local(): lax.all_to_all(outgoing.reshape(owners_total, CAP, components, span_cells...  12.7 us
    all_to_all x1, starting transfers between devices, local(): lax.all_to_all(outgoing.reshape(owners_total, CAP, components, span_cells...  6.32 us
    all_to_all x1, starting transfers between devices, local(): lax.all_to_all(slot_tags.reshape(owners_total, CAP), 'blk', split_axis=0,...  6.22 us
    unnamed x10, local copies, waits for them, and re-layouts  4.37 us
    dot_general x1, matrix products, local(): jnp.einsum('pk,kbx->pbx', own_columns, flattened, precision=highest)  4.32 us
  transfers between devices with their start and end apart: 5, of which 3 were waited for; matrix products, arithmetic and copies ran while one was open for 8% of the time, Pallas kernels for 0%

commit v1 on v0

v1 whole, which is shorter than its diff:
```python
import functools

import jax
import jax.numpy as jnp
from jax import lax
from jax.experimental import pallas as pl
from jax.experimental.pallas import tpu as pltpu
from jax.sharding import PartitionSpec as P

CAP = 2
MESH = pl.DeviceIdType.MESH
LAG = 2


def split(x):
    high = x.astype(jnp.bfloat16)
    low = (x - high.astype(jnp.float32)).astype(jnp.bfloat16)
    return high, low


def dot(a, b):
    return lax.dot_general(a, b, (((1,), (0,)), ((), ())), preferred_element_type=jnp.float32)


def dot_t(a, b):
    return lax.dot_general(a, b, (((1,), (1,)), ((), ())), preferred_element_type=jnp.float32)


def iota(shape, dim):
    return lax.broadcasted_iota(jnp.int32, shape, dim)


def to_column(row):
    n = row.shape[1]
    eye = iota((n, n), 0) == iota((n, n), 1)
    return jnp.sum(jnp.where(eye, row, 0), axis=1, keepdims=True)


def kernel(
    n_pitch, n_blk, step, group,
    flux, pitch_op, span_op, row_ref, owner_ref, slot_ref, count_ref,
    out, update, mask,
    low, high, gathered, outgoing, arrived, tags_out, tags_in, lhs, span3, pick,
    low_send, low_recv, high_send, high_recv, y_send, y_recv, row_send, row_recv, tag_send, tag_recv,
):
    comps, lines, cells = flux.shape
    pitch_all = pitch_op.shape[1]
    store = update.shape[1]
    steps = comps // step
    groups = steps // group
    slots = CAP * n_blk
    block_rows = arrived.shape[1] // n_blk
    g = lax.axis_index("pitch")
    me = lax.axis_index("blk")
    f32 = jnp.float32

    def blk_at(k):
        return lax.rem(me + k, n_blk)

    def pitch_at(k):
        return lax.rem(g + k, n_pitch)

    barrier = pltpu.get_barrier_semaphore()

    @pl.loop(1, n_blk)
    def _(k):
        pl.semaphore_signal(barrier, inc=1, device_id={"blk": blk_at(k)}, device_id_type=MESH)

    @pl.loop(1, n_pitch)
    def _(k):
        pl.semaphore_signal(barrier, inc=1, device_id={"pitch": pitch_at(k)}, device_id_type=MESH)

    pl.semaphore_wait(barrier, n_blk - 1 + n_pitch - 1)

    def up(i):
        part = pl.ds(i * step, step)
        return pltpu.make_async_remote_copy(
            src_ref=flux.at[part], dst_ref=low.at[part],
            send_sem=low_send.at[i], recv_sem=low_recv.at[i],
            device_id={"blk": jnp.minimum(me + 1, n_blk - 1)}, device_id_type=MESH,
        )

    def down(i):
        part = pl.ds(i * step, step)
        return pltpu.make_async_remote_copy(
            src_ref=flux.at[part], dst_ref=high.at[part],
            send_sem=high_send.at[i], recv_sem=high_recv.at[i],
            device_id={"blk": jnp.maximum(me - 1, 0)}, device_id_type=MESH,
        )

    own_lines = pl.ds(pl.multiple_of(g * lines, lines), lines)

    def across(i, k):
        ref = gathered.at[pl.ds(i * step, step), own_lines]
        return pltpu.make_async_remote_copy(
            src_ref=ref, dst_ref=ref, send_sem=y_send.at[i, k], recv_sem=y_recv.at[i, k],
            device_id={"pitch": pitch_at(k)}, device_id_type=MESH,
        )

    def rows_to(j, k):
        return pltpu.make_async_remote_copy(
            src_ref=outgoing.at[j, pl.ds(pl.multiple_of(blk_at(k) * block_rows, 8), block_rows)],
            dst_ref=arrived.at[j, pl.ds(pl.multiple_of(me * block_rows, 8), block_rows)],
            send_sem=row_send.at[j, k], recv_sem=row_recv.at[j, k],
            device_id={"blk": blk_at(k)}, device_id_type=MESH,
        )

    def tags_to(k):
        return pltpu.make_async_remote_copy(
            src_ref=tags_out, dst_ref=tags_in.at[me],
            send_sem=tag_send.at[k], recv_sem=tag_recv.at[k],
            device_id={"blk": blk_at(k)}, device_id_type=MESH,
        )

    @pl.loop(0, steps)
    def _(i):
        @pl.when(me < n_blk - 1)
        def _():
            up(i).start()

        @pl.when(me > 0)
        def _():
            down(i).start()

    @pl.when(me == 0)
    def _():
        low[...] = jnp.zeros_like(low)

    @pl.when(me == n_blk - 1)
    def _():
        high[...] = jnp.zeros_like(high)

    entries = owner_ref.shape[1]
    owner = owner_ref[...]
    same = (to_column(owner) == owner) & (iota((entries, entries), 0) < iota((entries, entries), 1))
    rank = jnp.sum(same.astype(jnp.int32), axis=0, keepdims=True)
    live = (iota((1, entries), 1) < count_ref[...]) & (rank < CAP)
    target = jnp.where(live, rank * n_blk + owner, -1)
    here = iota((slots, entries), 0) == target
    line = jnp.sum(jnp.where(here, row_ref[...] + 1, 0), axis=1, keepdims=True) - 1
    choose = (iota((slots, lines), 1) == line).astype(f32).astype(jnp.bfloat16)
    there = to_column(target) == iota((entries, 128), 1)
    tag = jnp.sum(jnp.where(there, to_column(slot_ref[...]) + 1, 0), axis=0, keepdims=True) - 1
    tags_out[...] = jnp.broadcast_to(tag, tags_out.shape)
    tags_in[me] = jnp.broadcast_to(tag, tags_out.shape)

    @pl.loop(1, n_blk)
    def _(k):
        tags_to(k).start()

    a_high, a_low = split(pitch_op[...])
    a_high = jnp.concatenate([a_high.astype(f32), dot(choose, a_high)], axis=0).astype(jnp.bfloat16)
    a_low = jnp.concatenate([a_low.astype(f32), dot(choose, a_low)], axis=0).astype(jnp.bfloat16)
    lhs[...] = jnp.concatenate([a_high, a_high, a_low], axis=1)
    b_high, b_low = split(span_op[...])
    span3[...] = jnp.concatenate([b_high, b_low, b_high], axis=1)

    def place(j):
        @pl.loop(1, n_blk)
        def _(k):
            rows_to(j, k).wait_recv()

        both = pick[...]
        for q in range(group * step):
            parts = [
                arrived[j, pl.ds(q * CAP + c, n_blk, stride=block_rows), :] for c in range(CAP)
            ]
            top, rest = split(jnp.concatenate(parts, axis=0))
            update[j * (group * step) + q] = dot(both, jnp.concatenate([top, rest], axis=0))

    @pl.loop(0, steps + LAG)
    def _(i):
        @pl.when(i < steps)
        def _():
            @pl.when(me > 0)
            def _():
                up(i).wait_recv()

            @pl.when(me < n_blk - 1)
            def _():
                down(i).wait_recv()

            part = pl.ds(i * step, step)
            residual = 0.25 * high[part] - 0.75 * low[part] + 0.5 * flux[part]
            r_high, r_low = split(residual.reshape(step * lines, cells))
            y = dot_t(jnp.concatenate([r_high, r_high, r_low], axis=1), span3[...])
            gathered[part, own_lines, :] = y.reshape(step, lines, cells)

            @pl.loop(1, n_pitch)
            def _(k):
                across(i, k).start()

        @pl.when(i >= LAG)
        def _():
            m = i - LAG

            @pl.loop(1, n_pitch)
            def _(k):
                across(m, k).wait_recv()

            j = m // group
            inner = lax.rem(m, group) * step
            y_high, y_low = split(gathered[pl.ds(m * step, step)])
            stacked = jnp.concatenate([y_high, y_low, y_high], axis=1)
            wide = jnp.concatenate([stacked[q] for q in range(step)], axis=1)
            result = dot(lhs[...], wide)
            for q in range(step):
                piece = result[:, q * cells : (q + 1) * cells]
                out[m * step + q] = piece[:lines]
                for c in range(CAP):
                    first = lines + c * n_blk
                    outgoing[j, pl.ds((inner + q) * CAP + c, n_blk, stride=block_rows), :] = piece[
                        first : first + n_blk
                    ]

            @pl.when(lax.rem(m, group) == group - 1)
            def _():
                @pl.loop(1, n_blk)
                def _(k):
                    rows_to(j, k).start()

                own = pl.ds(pl.multiple_of(me * block_rows, 8), block_rows)
                arrived[j, own, :] = outgoing[j, own, :]

                @pl.when(j == 0)
                def _():
                    @pl.loop(1, n_blk)
                    def _(k):
                        tags_to(k).wait_recv()

                    tags = tags_in[:, 0, :]
                    lanes = iota((n_blk, 128), 1)
                    found = [
                        jnp.sum(jnp.where(lanes == c * n_blk + me, tags, 0), axis=1, keepdims=True)
                        for c in range(CAP)
                    ]
                    spots = iota((n_blk, slots), 1)
                    senders = iota((n_blk, slots), 0)
                    tag_of = jnp.zeros((n_blk, slots), jnp.int32)
                    for c in range(CAP):
                        tag_of = jnp.where(spots == senders + c * n_blk, found[c], tag_of)
                    slot_of = jnp.sum(tag_of, axis=0, keepdims=True)
                    hits = (iota((store, slots), 0) == slot_of).astype(f32)
                    pick[...] = jnp.concatenate([hits, hits], axis=1).astype(jnp.bfloat16)
                    mask[...] = jnp.broadcast_to(jnp.sum(hits, axis=1, keepdims=True), mask.shape)

                @pl.when(j >= 1)
                def _():
                    place(j - 1)

    place(groups - 1)

    @pl.loop(0, steps)
    def _(i):
        @pl.when(me < n_blk - 1)
        def _():
            up(i).wait_send()

        @pl.when(me > 0)
        def _():
            down(i).wait_send()

        @pl.loop(1, n_pitch)
        def _(k):
            across(i, k).wait_send()

    @pl.loop(1, n_blk)
    def _(k):
        tags_to(k).wait_send()

        @pl.loop(0, groups)
        def _(j):
            rows_to(j, k).wait_send()


def local(
    n_pitch, n_blk,
    flux, pitch_inverse, span_inverse, store_old, send_row, send_owner, send_slot, send_count,
):
    lines, _, comps, cells = flux.shape
    pitch_all = pitch_inverse.shape[2]
    store = store_old.shape[2]
    step = next(s for s in (5, 4, 3, 2, 1) if comps % s == 0)
    steps = comps // step
    group = next(s for s in (3, 2, 1) if steps % s == 0)
    groups = steps // group
    slots = CAP * n_blk
    block_rows = -(-(CAP * group * step) // 8) * 8
    f32, dma = jnp.float32, pltpu.SemaphoreType.DMA
    vmem = pl.BlockSpec(memory_space=pltpu.VMEM)
    smoothed, update, mask = pl.pallas_call(
        functools.partial(kernel, n_pitch, n_blk, step, group),
        out_shape=(
            jax.ShapeDtypeStruct((comps, lines, cells), f32),
            jax.ShapeDtypeStruct((comps, store, cells), f32),
            jax.ShapeDtypeStruct((store, 128), f32),
        ),
        in_specs=[vmem] * 7,
        out_specs=(vmem,) * 3,
        scratch_shapes=[
            pltpu.VMEM((comps, lines, cells), f32),
            pltpu.VMEM((comps, lines, cells), f32),
            pltpu.VMEM((comps, pitch_all, cells), f32),
            pltpu.VMEM((groups, n_blk * block_rows, cells), f32),
            pltpu.VMEM((groups, n_blk * block_rows, cells), f32),
            pltpu.VMEM((8, 128), jnp.int32),
            pltpu.VMEM((n_blk, 8, 128), jnp.int32),
            pltpu.VMEM((lines + slots, 3 * pitch_all), jnp.bfloat16),
            pltpu.VMEM((cells, 3 * cells), jnp.bfloat16),
            pltpu.VMEM((store, 2 * slots), jnp.bfloat16),
            dma((steps,)),
            dma((steps,)),
            dma((steps,)),
            dma((steps,)),
            dma((steps, n_pitch)),
            dma((steps, n_pitch)),
            dma((groups, n_blk)),
            dma((groups, n_blk)),
            dma((n_blk,)),
            dma((n_blk,)),
        ],
        compiler_params=pltpu.CompilerParams(
            collective_id=0, has_side_effects=True, vmem_limit_bytes=40 * 2**20
        ),
    )(
        jnp.transpose(flux[:, 0], (1, 0, 2)),
        pitch_inverse[0],
        span_inverse[0],
        send_row[0],
        send_owner[0],
        send_slot[0],
        send_count,
    )
    hit = mask[:, :1, None] > 0
    storage = jnp.where(hit, jnp.transpose(update, (1, 0, 2)), store_old[0, 0].astype(f32))
    return jnp.transpose(smoothed, (1, 0, 2))[:, None], storage[None, None]


def solution(mesh):
    return jax.shard_map(
        functools.partial(local, mesh.shape["pitch"], mesh.shape["blk"]),
        mesh=mesh,
        in_specs=(
            P("pitch", "blk", None, None),
            P("blk", "pitch", None),
            P("blk", None, None),
            P("pitch", "blk", None, None, None),
            P("pitch", "blk", None),
            P("pitch", "blk", None),
            P("pitch", "blk", None),
            P("pitch", "blk"),
        ),
        out_specs=(P("pitch", "blk", None, None), P("pitch", "blk", None, None, None)),
        check_vma=False,
    )
```

time: 150 us -> 74.4 us (0.50); the launches traced: 148 us -> 74.3 us
  waiting for transfers between devices: 72.6 us -> 0 us
  Pallas kernels: 0 us -> 67.5 us
  starting transfers between devices: 18.2 us -> 0 us
  other arithmetic: 17.4 us -> 1.15 us
  between operations: 14.9 us -> 1.39 us
  local copies, waits for them, and re-layouts: 14.6 us -> 4.25 us
  matrix products: 5.93 us -> 0 us
  blocking collectives: 4.12 us -> 0 us
    pallas_call x0 -> x1, Pallas kernels: none -> 67.5 us  [local(): pl.pallas_call(functools.partial(kernel, n_pitch, n_blk, step, group), ou...]
    reduce_scatter x1 -> x0, waiting for transfers between devices: 32.9 us -> none  [local(): lax.psum_scatter(jnp.einsum('pk,kbx->pbx', own_columns, flattened, precis...]
    ppermute x2 -> x0, waiting for transfers between devices: 27 us -> none  [the longest x1 27 us: with_halo(): lax.ppermute(lax.slice_in_dim(block, 0, width, axis=dim), axis, backward)]
    add x1 -> x0, other arithmetic: 16.3 us -> none  [local(): residual = 0.25 * padded[:, 2:] - 0.75 * padded[:, :-2] + 0.5 * flux]
    all_to_all x2 -> x0, waiting for transfers between devices: 12.7 us -> none  [the longest x1 12.7 us: local(): lax.all_to_all(outgoing.reshape(owners_total, CAP, components, span_cells...]
    all_to_all x2 -> x0, starting transfers between devices: 12.5 us -> none  [the longest x1 6.32 us: local(): lax.all_to_all(outgoing.reshape(owners_total, CAP, components, span_cells...]
    dot_general x2 -> x0, matrix products: 5.93 us -> none  [the longest x1 4.32 us: local(): jnp.einsum('pk,kbx->pbx', own_columns, flattened, precision=highest)]
    ppermute x2 -> x0, starting transfers between devices: 5.63 us -> none  [the longest x1 3.05 us: with_halo(): lax.ppermute(lax.slice_in_dim(block, block.shape[dim] - width, None, axis...]
  transfers between devices with their start and end apart: 5 -> 0, of which waited for: 3 -> 0; matrix products, arithmetic and copies ran while one was open for 8% -> 0% of each run, Pallas kernels for 0% -> 0%
where the time goes in v1:
time: 74.4 us; the launch traced here: 74.3 us
  Pallas kernels  67.5 us (91%)
  local copies, waits for them, and re-layouts  4.25 us (6%)
  between operations  1.39 us (2%)
  other arithmetic  1.15 us (2%)
    pallas_call x1, Pallas kernels, local(): pl.pallas_call(functools.partial(kernel, n_pitch, n_blk, step, group), ou...  67.5 us
    unnamed x14, local copies, waits for them, and re-layouts  4.25 us

profile of v1, /device:TPU:25, one launch (start us, length us, event | category | flops | bytes accessed | tf_op | source)
XLA Modules:
  0.0 74.3 jit_solution(4609669080302281783)
XLA Ops:
  1.3 0.0 copy-start
  1.3 0.0 copy-start.1
  1.3 0.0 copy-start.2
  1.3 0.0 copy-start.3
  1.3 0.0 copy-start.4
  1.3 1.6 %copy.15 = f32[64,1,45,128]{3,0,2,1:T(8,128)S(1)} copy(f32[64,1,45,128]{3,1,2,0:T(1,128)} %param.8) | data formatting | bytes 2949120 | tf_op args[0]
  2.9 0.0 copy-done
  2.9 0.0 copy-done.1
  3.0 0.0 copy-done.2
  3.0 0.0 copy-done.3
  3.0 0.0 copy-done.4
  3.0 67.5 %shard_map.95 = (f32[45,64,128]{2,1,0:T(8,128)S(1)}, f32[45,32,128]{2,1,0:T(8,128)S(1)}, f32[32,128]{1,0:T(8,128)S(1)}) custom-call(f32[45,64,128]{2,1,0:T(8,128)S(1)} %bitcast.20, f32[64,128]{1,0:T(8,128)S(1)} %bitcast.23, f32[128,128]{1,0:T(8,128)S(1)} %bitcast.22, s32[1,16]{1,0:T(1,128)S(1)} %bitcast.24, s32[1,16]{1,0:T(1,128)S(1)} %bitcast.25, ...), custom_call_target="tpu_custom_call" | custom-call | tf_op jit(solution)/shard_map/pallas_call | solution.py:291
  70.5 0.0 copy-start.5
  70.5 2.6 %copy.13 = f32[64,1,45,128]{3,1,2,0:T(1,128)} copy(f32[64,1,45,128]{3,0,2,1:T(8,128)S(1)} %bitcast.21) | data formatting | bytes 2949120
  73.1 0.1 fusion.1
  73.2 0.0 copy-done.5
  73.2 1.0 %fusion = f32[1,1,32,45,128]{4,2,3,1,0:T(8,128)} fusion(f32[45,32,128]{2,1,0:T(8,128)S(1)} %get-tuple-element.7, bf16[1,1,32,45,128]{4,2,3,1,0:T(8,128)(2,1)S(1)} %copy-done.5, pred[32]{0:T(512)(128)(4,1)S(1)} %fusion.1), kind=kLoop, calls=%fused_computation.2 | loop fusion | flops 368640 | bytes 1843232 | tf_op jit(solution)/shard_map/broadcast_in_dim | solution.py:336
Async XLA Ops:
  1.3 1.7 %copy-start = (f32[1,128,128]{2,1,0:T(8,128)S(1)}, f32[1,128,128]{2,1,0:T(8,128)}, u32[]{:S(2)}) copy-start(f32[1,128,128]{2,1,0:T(8,128)} %param.10) | copy-start | bytes 196612
  1.3 1.7 %copy-start.1 = (f32[1,64,128]{2,1,0:T(8,128)S(1)}, f32[1,64,128]{2,1,0:T(8,128)}, u32[]{:S(2)}) copy-start(f32[1,64,128]{2,1,0:T(8,128)} %param.9) | copy-start | bytes 98308
  1.3 1.7 %copy-start.2 = (s32[1,1,16]{2,1,0:T(1,128)S(1)}, s32[1,1,16]{2,1,0:T(1,128)}, u32[]{:S(2)}) copy-start(s32[1,1,16]{2,1,0:T(1,128)} %param.12) | copy-start | bytes 196
  1.3 1.7 %copy-start.3 = (s32[1,1,16]{2,1,0:T(1,128)S(1)}, s32[1,1,16]{2,1,0:T(1,128)}, u32[]{:S(2)}) copy-start(s32[1,1,16]{2,1,0:T(1,128)} %param.13) | copy-start | bytes 196
  1.3 1.7 %copy-start.4 = (s32[1,1,16]{2,1,0:T(1,128)S(1)}, s32[1,1,16]{2,1,0:T(1,128)}, u32[]{:S(2)}) copy-start(s32[1,1,16]{2,1,0:T(1,128)} %param.14) | copy-start | bytes 196
  70.5 2.8 %copy-start.5 = (bf16[1,1,32,45,128]{4,2,3,1,0:T(8,128)(2,1)S(1)}, bf16[1,1,32,45,128]{4,2,3,1,0:T(8,128)(2,1)}, u32[]{:S(2)}) copy-start(bf16[1,1,32,45,128]{4,2,3,1,0:T(8,128)(2,1)} %param.11) | copy-start | bytes 1105924

commit v2 on v1

--- a/solution.py
+++ b/solution.py
@@ -9,7 +9,8 @@
 
 CAP = 2
 MESH = pl.DeviceIdType.MESH
-LAG = 2
+LAG = 3
+AHEAD = 2
 
 
 def split(x):
@@ -38,9 +39,9 @@
 
 def kernel(
     n_pitch, n_blk, step, group,
-    flux, pitch_op, span_op, row_ref, owner_ref, slot_ref, count_ref,
+    flux_rows, pitch_op, span_op, row_ref, owner_ref, slot_ref, count_ref,
     out, update, mask,
-    low, high, gathered, outgoing, arrived, tags_out, tags_in, lhs, span3, pick,
+    flux, low, high, gathered, outgoing, arrived, tags_out, tags_in, lhs, span3, pick,
     low_send, low_recv, high_send, high_recv, y_send, y_recv, row_send, row_recv, tag_send, tag_recv,
 ):
     comps, lines, cells = flux.shape
@@ -70,7 +71,8 @@
     def _(k):
         pl.semaphore_signal(barrier, inc=1, device_id={"pitch": pitch_at(k)}, device_id_type=MESH)
 
-    pl.semaphore_wait(barrier, n_blk - 1 + n_pitch - 1)
+    for q in range(comps):
+        flux[q] = flux_rows[pl.ds(q, lines, stride=comps), :]
 
     def up(i):
         part = pl.ds(i * step, step)
@@ -93,7 +95,7 @@
     def across(i, k):
         ref = gathered.at[pl.ds(i * step, step), own_lines]
         return pltpu.make_async_remote_copy(
-            src_ref=ref, dst_ref=ref, send_sem=y_send.at[i, k], recv_sem=y_recv.at[i, k],
+            src_ref=ref, dst_ref=ref, send_sem=y_send.at[k], recv_sem=y_recv.at[i, k],
             device_id={"pitch": pitch_at(k)}, device_id_type=MESH,
         )
 
@@ -101,26 +103,16 @@
         return pltpu.make_async_remote_copy(
             src_ref=outgoing.at[j, pl.ds(pl.multiple_of(blk_at(k) * block_rows, 8), block_rows)],
             dst_ref=arrived.at[j, pl.ds(pl.multiple_of(me * block_rows, 8), block_rows)],
-            send_sem=row_send.at[j, k], recv_sem=row_recv.at[j, k],
+            send_sem=row_send, recv_sem=row_recv.at[j],
             device_id={"blk": blk_at(k)}, device_id_type=MESH,
         )
 
     def tags_to(k):
         return pltpu.make_async_remote_copy(
             src_ref=tags_out, dst_ref=tags_in.at[me],
-            send_sem=tag_send.at[k], recv_sem=tag_recv.at[k],
+            send_sem=tag_send, recv_sem=tag_recv,
             device_id={"blk": blk_at(k)}, device_id_type=MESH,
         )
-
-    @pl.loop(0, steps)
-    def _(i):
-        @pl.when(me < n_blk - 1)
-        def _():
-            up(i).start()
-
-        @pl.when(me > 0)
-        def _():
-            down(i).start()
 
     @pl.when(me == 0)
     def _():
@@ -144,10 +136,6 @@
     tags_out[...] = jnp.broadcast_to(tag, tags_out.shape)
     tags_in[me] = jnp.broadcast_to(tag, tags_out.shape)
 
-    @pl.loop(1, n_blk)
-    def _(k):
-        tags_to(k).start()
-
     a_high, a_low = split(pitch_op[...])
     a_high = jnp.concatenate([a_high.astype(f32), dot(choose, a_high)], axis=0).astype(jnp.bfloat16)
     a_low = jnp.concatenate([a_low.astype(f32), dot(choose, a_low)], axis=0).astype(jnp.bfloat16)
@@ -155,11 +143,50 @@
     b_high, b_low = split(span_op[...])
     span3[...] = jnp.concatenate([b_high, b_low, b_high], axis=1)
 
+    pl.semaphore_wait(barrier, n_blk - 1 + n_pitch - 1)
+
+    def halo_start(i):
+        @pl.when(me < n_blk - 1)
+        def _():
+            up(i).start()
+
+        @pl.when(me > 0)
+        def _():
+            down(i).start()
+
+    def halo_sent(i):
+        @pl.when(me < n_blk - 1)
+        def _():
+            up(i).wait_send()
+
+        @pl.when(me > 0)
+        def _():
+            down(i).wait_send()
+
+    for i in range(min(AHEAD, steps)):
+        halo_start(i)
+
+    @pl.loop(1, n_blk)
+    def _(k):
+        tags_to(k).start()
+
+    def all_rows(j):
+        part = pl.ds(0, (n_blk - 1) * block_rows)
+        return pltpu.make_async_remote_copy(
+            src_ref=outgoing.at[j, part], dst_ref=arrived.at[j, part],
+            send_sem=row_send, recv_sem=row_recv.at[j],
+            device_id={"blk": blk_at(1)}, device_id_type=MESH,
+        )
+
+    def all_tags():
+        part = tags_in.at[pl.ds(0, n_blk - 1)]
+        return pltpu.make_async_remote_copy(
+            src_ref=part, dst_ref=part, send_sem=tag_send, recv_sem=tag_recv,
+            device_id={"blk": blk_at(1)}, device_id_type=MESH,
+        )
+
     def place(j):
-        @pl.loop(1, n_blk)
-        def _(k):
-            rows_to(j, k).wait_recv()
-
+        all_rows(j).wait_recv()
         both = pick[...]
         for q in range(group * step):
             parts = [
@@ -179,6 +206,12 @@
             @pl.when(me < n_blk - 1)
             def _():
                 down(i).wait_recv()
+
+            halo_sent(i)
+
+            @pl.when(i + AHEAD < steps)
+            def _():
+                halo_start(i + AHEAD)
 
             part = pl.ds(i * step, step)
             residual = 0.25 * high[part] - 0.75 * low[part] + 0.5 * flux[part]
@@ -206,7 +239,7 @@
             result = dot(lhs[...], wide)
             for q in range(step):
                 piece = result[:, q * cells : (q + 1) * cells]
-                out[m * step + q] = piece[:lines]
+                out[pl.ds(m * step + q, lines, stride=comps), :] = piece[:lines]
                 for c in range(CAP):
                     first = lines + c * n_blk
                     outgoing[j, pl.ds((inner + q) * CAP + c, n_blk, stride=block_rows), :] = piece[
@@ -224,10 +257,7 @@
 
                 @pl.when(j == 0)
                 def _():
-                    @pl.loop(1, n_blk)
-                    def _(k):
-                        tags_to(k).wait_recv()
-
+                    all_tags().wait_recv()
                     tags = tags_in[:, 0, :]
                     lanes = iota((n_blk, 128), 1)
                     found = [
@@ -250,27 +280,21 @@
 
     place(groups - 1)
 
-    @pl.loop(0, steps)
-    def _(i):
-        @pl.when(me < n_blk - 1)
-        def _():
-            up(i).wait_send()
-
-        @pl.when(me > 0)
-        def _():
-            down(i).wait_send()
-
-        @pl.loop(1, n_pitch)
-        def _(k):
-            across(i, k).wait_send()
-
-    @pl.loop(1, n_blk)
+    @pl.loop(1, n_pitch)
     def _(k):
-        tags_to(k).wait_send()
-
-        @pl.loop(0, groups)
-        def _(j):
-            rows_to(j, k).wait_send()
+        ref = gathered.at[:, own_lines]
+        pltpu.make_async_remote_copy(
+            src_ref=ref, dst_ref=ref, send_sem=y_send.at[k], recv_sem=y_recv.at[0, k],
+            device_id={"pitch": pitch_at(k)}, device_id_type=MESH,
+        ).wait_send()
+
+    all_tags().wait_send()
+    part = pl.ds(0, (n_blk - 1) * block_rows)
+    pltpu.make_async_remote_copy(
+        src_ref=outgoing.at[:, part], dst_ref=arrived.at[:, part],
+        send_sem=row_send, recv_sem=row_recv.at[0],
+        device_id={"blk": blk_at(1)}, device_id_type=MESH,
+    ).wait_send()
 
 
 def local(
@@ -291,13 +315,14 @@
     smoothed, update, mask = pl.pallas_call(
         functools.partial(kernel, n_pitch, n_blk, step, group),
         out_shape=(
-            jax.ShapeDtypeStruct((comps, lines, cells), f32),
+            jax.ShapeDtypeStruct((lines * comps, cells), f32),
             jax.ShapeDtypeStruct((comps, store, cells), f32),
             jax.ShapeDtypeStruct((store, 128), f32),
         ),
         in_specs=[vmem] * 7,
         out_specs=(vmem,) * 3,
         scratch_shapes=[
+            pltpu.VMEM((comps, lines, cells), f32),
             pltpu.VMEM((comps, lines, cells), f32),
             pltpu.VMEM((comps, lines, cells), f32),
             pltpu.VMEM((comps, pitch_all, cells), f32),
@@ -312,18 +337,18 @@
             dma((steps,)),
             dma((steps,)),
             dma((steps,)),
+            dma((n_pitch,)),
             dma((steps, n_pitch)),
-            dma((steps, n_pitch)),
-            dma((groups, n_blk)),
-            dma((groups, n_blk)),
-            dma((n_blk,)),
-            dma((n_blk,)),
+            dma,
+            dma((groups,)),
+            dma,
+            dma,
         ],
         compiler_params=pltpu.CompilerParams(
             collective_id=0, has_side_effects=True, vmem_limit_bytes=40 * 2**20
         ),
     )(
-        jnp.transpose(flux[:, 0], (1, 0, 2)),
+        flux.reshape(lines * comps, cells),
         pitch_inverse[0],
         span_inverse[0],
         send_row[0],
@@ -333,7 +358,7 @@
     )
     hit = mask[:, :1, None] > 0
     storage = jnp.where(hit, jnp.transpose(update, (1, 0, 2)), store_old[0, 0].astype(f32))
-    return jnp.transpose(smoothed, (1, 0, 2))[:, None], storage[None, None]
+    return smoothed.reshape(flux.shape), storage[None, None]
 
 
 def solution(mesh):

time: 74.4 us -> 63.6 us (0.85)
  Pallas kernels: 67.5 us -> 54.8 us
  local copies, waits for them, and re-layouts: 4.25 us -> 6.04 us
    pallas_call x1, Pallas kernels: 67.5 us -> 54.8 us  [local(): pl.pallas_call(functools.partial(kernel, n_pitch, n_blk, step, group), ou...]
    unnamed x14 -> x15, local copies, waits for them, and re-layouts: 4.25 us -> 6.04 us
where the time goes in v2:
time: 63.6 us; the launch traced here: 63.3 us
  Pallas kernels  54.8 us (86%)
  local copies, waits for them, and re-layouts  6.04 us (9%)
  between operations  1.31 us (2%)
  other arithmetic  1.15 us (2%)
    pallas_call x1, Pallas kernels, local(): pl.pallas_call(functools.partial(kernel, n_pitch, n_blk, step, group), ou...  54.8 us
    unnamed x15, local copies, waits for them, and re-layouts  6.04 us

profile of v2, /device:TPU:25, one launch (start us, length us, event | category | flops | bytes accessed | tf_op | source)
XLA Modules:
  0.0 63.3 jit_solution(10888855380414192659)
XLA Ops:
  1.3 0.0 copy-start
  1.3 1.4 %copy-done = f32[64,1,45,128]{3,1,2,0:T(1,128)S(1)} copy-done((f32[64,1,45,128]{3,1,2,0:T(1,128)S(1)}, f32[64,1,45,128]{3,1,2,0:T(1,128)}, u32[]{:S(2)}) %copy-start) | copy-done | bytes 1474584
  2.7 0.0 copy-start.1
  2.7 0.8 %copy-done.1 = f32[1,128,128]{2,1,0:T(8,128)S(1)} copy-done((f32[1,128,128]{2,1,0:T(8,128)S(1)}, f32[1,128,128]{2,1,0:T(8,128)}, u32[]{:S(2)}) %copy-start.1) | copy-done | bytes 65560
  3.5 0.0 copy-start.2
  3.5 0.8 %copy-done.2 = f32[1,64,128]{2,1,0:T(8,128)S(1)} copy-done((f32[1,64,128]{2,1,0:T(8,128)S(1)}, f32[1,64,128]{2,1,0:T(8,128)}, u32[]{:S(2)}) %copy-start.2) | copy-done | bytes 32792
  4.3 0.0 copy-start.3
  4.3 0.7 %copy-done.3 = s32[1,1,16]{2,1,0:T(1,128)S(1)} copy-done((s32[1,1,16]{2,1,0:T(1,128)S(1)}, s32[1,1,16]{2,1,0:T(1,128)}, u32[]{:S(2)}) %copy-start.3) | copy-done | bytes 88
  4.9 0.0 copy-start.4
  4.9 0.7 %copy-done.4 = s32[1,1,16]{2,1,0:T(1,128)S(1)} copy-done((s32[1,1,16]{2,1,0:T(1,128)S(1)}, s32[1,1,16]{2,1,0:T(1,128)}, u32[]{:S(2)}) %copy-start.4) | copy-done | bytes 88
  5.6 0.0 copy-start.5
  5.6 0.7 %copy-done.5 = s32[1,1,16]{2,1,0:T(1,128)S(1)} copy-done((s32[1,1,16]{2,1,0:T(1,128)S(1)}, s32[1,1,16]{2,1,0:T(1,128)}, u32[]{:S(2)}) %copy-start.5) | copy-done | bytes 88
  6.2 0.0 copy-start.6
  6.2 54.8 %shard_map.95 = (f32[2880,128]{1,0:T(8,128)S(1)}, f32[45,32,128]{2,1,0:T(8,128)S(1)}, f32[32,128]{1,0:T(8,128)S(1)}) custom-call(f32[2880,128]{1,0:T(8,128)S(1)} %bitcast.14, f32[64,128]{1,0:T(8,128)S(1)} %bitcast.17, f32[128,128]{1,0:T(8,128)S(1)} %bitcast.16, s32[1,16]{1,0:T(1,128)S(1)} %bitcast.18, s32[1,16]{1,0:T(1,128)S(1)} %bitcast.19, ...), custom_call_target="tpu_custom_call" | custom-call | tf_op jit(solution)/shard_map/pallas_call | solution.py:315
  61.1 0.1 fusion.1
  61.2 0.0 copy-done.6
  61.2 1.0 %fusion = f32[1,1,32,45,128]{4,2,3,1,0:T(8,128)} fusion(f32[45,32,128]{2,1,0:T(8,128)S(1)} %get-tuple-element.7, bf16[1,1,32,45,128]{4,2,3,1,0:T(8,128)(2,1)S(1)} %copy-done.6, pred[32]{0:T(512)(128)(4,1)S(1)} %fusion.1), kind=kLoop, calls=%fused_computation.1 | loop fusion | flops 368640 | bytes 1843232 | tf_op jit(solution)/shard_map/broadcast_in_dim | solution.py:361
  62.2 1.1 %copy.14 = f32[64,1,45,128]{3,1,2,0:T(1,128)} copy(f32[64,1,45,128]{3,1,2,0:T(1,128)S(1)} %bitcast.15) | data formatting | bytes 2949120
Async XLA Ops:
  1.3 1.4 %copy-start = (f32[64,1,45,128]{3,1,2,0:T(1,128)S(1)}, f32[64,1,45,128]{3,1,2,0:T(1,128)}, u32[]{:S(2)}) copy-start(f32[64,1,45,128]{3,1,2,0:T(1,128)} %param.8) | copy-start | bytes 4423684
  2.7 0.8 %copy-start.1 = (f32[1,128,128]{2,1,0:T(8,128)S(1)}, f32[1,128,128]{2,1,0:T(8,128)}, u32[]{:S(2)}) copy-start(f32[1,128,128]{2,1,0:T(8,128)} %param.10) | copy-start | bytes 196612
  3.5 0.8 %copy-start.2 = (f32[1,64,128]{2,1,0:T(8,128)S(1)}, f32[1,64,128]{2,1,0:T(8,128)}, u32[]{:S(2)}) copy-start(f32[1,64,128]{2,1,0:T(8,128)} %param.9) | copy-start | bytes 98308
  4.3 0.7 %copy-start.3 = (s32[1,1,16]{2,1,0:T(1,128)S(1)}, s32[1,1,16]{2,1,0:T(1,128)}, u32[]{:S(2)}) copy-start(s32[1,1,16]{2,1,0:T(1,128)} %param.12) | copy-start | bytes 196
  4.9 0.7 %copy-start.4 = (s32[1,1,16]{2,1,0:T(1,128)S(1)}, s32[1,1,16]{2,1,0:T(1,128)}, u32[]{:S(2)}) copy-start(s32[1,1,16]{2,1,0:T(1,128)} %param.13) | copy-start | bytes 196
  5.6 0.7 %copy-start.5 = (s32[1,1,16]{2,1,0:T(1,128)S(1)}, s32[1,1,16]{2,1,0:T(1,128)}, u32[]{:S(2)}) copy-start(s32[1,1,16]{2,1,0:T(1,128)} %param.14) | copy-start | bytes 196
  6.2 55.0 %copy-start.6 = (bf16[1,1,32,45,128]{4,2,3,1,0:T(8,128)(2,1)S(1)}, bf16[1,1,32,45,128]{4,2,3,1,0:T(8,128)(2,1)}, u32[]{:S(2)}) copy-start(bf16[1,1,32,45,128]{4,2,3,1,0:T(8,128)(2,1)} %param.11) | copy-start | bytes 1105924
